TPU v7x, 256 devices: a whole 4x4x8 slice. The times are simulated.
256 devices in a mesh: gx: 16 (over y, z_lo), gy: 8 (over x, core), ga: 2 (over z_hi).
Axes of the slice: x: 4, y: 4, z: 8 (z_hi: 2, z_lo: 4; z = z_hi * 4 + z_lo), core: 2. Of those that a mesh axis runs over, the one named last changes fastest.
Arguments:
- thermal_anomaly: float32 [20, 1024, 4096], P(None, 'gy', ('gx', 'ga')), may hold values from -6 to 6
- sheared_current: float32 [2, 20, 1024, 4096], P(None, None, 'gy', ('gx', 'ga')), may hold values from -3 to 3
- mixing_coefficient: float32 [20, 1024, 4096], P(None, 'gy', ('gx', 'ga')), may hold values from 0.05 to 2
- surface_elevation: float32 [1024, 4096], P('gy', ('gx', 'ga')), may hold values from -2 to 2
- depth_integrated_current: float32 [2, 1024, 4096], P(None, 'gy', ('gx', 'ga')), may hold values from -3 to 3
- water_column_flag: int32 [1024, 4096], P('gy', ('gx', 'ga')), may hold values from 0 to 1
- wet_layer_counts: int32 [1024, 4096], P('gy', ('gx', 'ga')), may hold values from 1 to 20
Outputs:
- mixed: float32 [20, 1024, 4096], P(None, 'gy', ('gx', 'ga'))
- velocity_out: float32 [2, 20, 1024, 4096], P(None, None, 'gy', ('gx', 'ga'))
- height_out: float32 [1024, 4096], P('gy', ('gx', 'ga'))
- transport_out: float32 [2, 1024, 4096], P(None, 'gy', ('gx', 'ga'))
All inputs are finite; a program needn't handle non-finite values.
Results may differ from a plain program's by a relative error of at most 0.00002.
Values sent between devices are 32-bit elements; how exact they have to be, the bound alone decides.
No kernel may reach another device: no remote copies, remote signals or barrier semaphores. Data moves between devices by JAX's collectives and lax.ppermute only.
A program may use at most 64 MiB of HBM per device.

v0:
```python
import functools

import jax
import jax.numpy as jnp
from jax import lax
from jax.experimental import pallas as pl
from jax.experimental.pallas import tpu as pltpu
from jax.sharding import PartitionSpec as P

NSUB = 4
W = 8
TRANSPORT_SPEED = 0.2
MIXING = 1.0
THERMAL_EXPANSION = 0.05
TIMESTEP = 0.2
SUBSTEP = 0.3
GRAVITY = 1.0

AXES = ("gx", "gy", "ga")
FIELDS = 6
FLUX_LANE = 20
FIELD_LANE = 40
FOLD_LANE = 88
FOLD = 30
FOLD_ROWS = 32
GROUPS = 4
CHUNK = 32
SLABS = (4, 6, 6, 4)
UNROLL = 5
BACK_UNROLL = 4
VMEM_BYTES = 24 * 1024 * 1024
EDGES_VMEM = 54608 * 1024
COLUMNS_VMEM = 46 * 1024 * 1024


def lanes_of(shape):
    return lax.broadcasted_iota(jnp.int32, shape, len(shape) - 1)


def rows_of(shape):
    return lax.broadcasted_iota(jnp.int32, shape, len(shape) - 2)


def roll_lanes(x, amount):
    amount = amount % x.shape[-1] if isinstance(amount, int) else amount
    return x if isinstance(amount, int) and amount == 0 else pltpu.roll(x, amount, x.ndim - 1)


def roll_rows(x, amount):
    return pltpu.roll(x, amount % x.shape[-2], x.ndim - 2)


def coriolis_of(shape, row_start, total_rows):
    rows = (rows_of(shape) + row_start).astype(jnp.float32)
    return 0.3 + 0.4 * rows / total_rows


def fold(full):
    ny, nx = full.shape
    lane = lanes_of((FOLD_ROWS, nx))
    low = (ny - FOLD_ROWS) // 2
    middle = full[low : low + FOLD_ROWS]
    rest = jnp.concatenate([full[:low], full[low + FOLD_ROWS :]], axis=0)
    out = []
    for piece in range(3):
        part = rest[FOLD_ROWS * piece : FOLD_ROWS * (piece + 1)]
        out.append(jnp.where(lane < FOLD_LANE, part, roll_lanes(middle, FOLD_LANE - FOLD * piece)))
    return jnp.concatenate(out, axis=0)


def unfold(folded):
    rows, nx = folded.shape
    lane = lanes_of((FOLD_ROWS, nx))
    middle = jnp.zeros((FOLD_ROWS, nx), jnp.float32)
    for piece in range(3):
        part = folded[FOLD_ROWS * piece : FOLD_ROWS * (piece + 1)]
        mine = (lane >= FOLD * piece) & (lane < FOLD * (piece + 1))
        middle = jnp.where(mine, roll_lanes(part, FOLD * piece - FOLD_LANE), middle)
    return jnp.concatenate([folded[: rows // 2], middle, folded[rows // 2 :]], axis=0)


def edges_kernel(
    total_rows,
    thermal,
    current,
    surface,
    transport,
    flag,
    wet,
    first,
    second,
    to_first,
    to_second,
    packed,
    levels_here,
    sum_east,
    sum_north,
    force_east,
    force_north,
    ground,
    thermal_here,
    current_here,
    bars_here,
    edge_rows,
    packs,
    flag_here,
    wet_here,
    sems,
):
    depth, ny, nx = thermal.shape
    shape = (ny, nx)
    pad = -(-depth // 8) * 8
    masks = [
        pltpu.make_async_copy(flag, flag_here, sems.at[0]),
        pltpu.make_async_copy(wet, wet_here, sems.at[1]),
    ]
    slabs = []
    begin = 0
    for g, count in enumerate(SLABS):
        part = pl.ds(begin, count)
        begin += count
        slabs.append(
            [
                pltpu.make_async_copy(thermal.at[part], thermal_here.at[part], sems.at[3 + 3 * g]),
                pltpu.make_async_copy(current.at[0, part], current_here.at[0, part], sems.at[4 + 3 * g]),
                pltpu.make_async_copy(current.at[1, part], current_here.at[1, part], sems.at[5 + 3 * g]),
            ]
        )
    bars = [
        pltpu.make_async_copy(surface, bars_here.at[0], sems.at[3 + 3 * GROUPS]),
        pltpu.make_async_copy(transport, bars_here.at[pl.ds(1, 2)], sems.at[4 + 3 * GROUPS]),
    ]
    for copy in masks + [c for slab in slabs for c in slab] + bars:
        copy.start()
    lane = lanes_of(shape)
    zero = jnp.zeros(shape, jnp.float32)
    packs[0] = zero
    packs[1] = zero
    for ref in (sum_east, sum_north, force_east, force_north):
        ref[...] = zero
    edge_rows[...] = jnp.zeros(edge_rows.shape, jnp.float32)
    for copy in masks:
        copy.wait()
    levels_here[...] = (flag_here[...] * wet_here[...]).astype(jnp.float32)
    floor = pltpu.make_async_copy(levels_here, ground.at[0], sems.at[2])
    floor.start()

    def chunk(begin, count, start):
        inner = pl.ds(start, CHUNK)
        low, high = max(start - 8, 0), min(start + CHUNK + 8, ny)
        deep = levels_here[low:high]
        mine = slice(start - low, start - low + CHUNK)
        part = lanes_of((CHUNK, nx))
        row = rows_of((CHUNK, nx))
        totals = [ref[inner] for ref in (sum_east, sum_north, force_east, force_north)]
        east, west = packs[0, inner], packs[1, inner]
        for k in range(begin, begin + count):
            weight = jnp.maximum(deep[mine] - float(k), 0.0)
            mask = weight > 0.0
            wide = jnp.where(deep > float(k), thermal_here[k, low:high], 0.0)
            t = wide[mine]
            u = current_here[0, k, inner]
            v = current_here[1, k, inner]
            totals[0] += jnp.where(mask, u, 0.0)
            totals[1] += jnp.where(mask, v, 0.0)
            totals[2] += weight * (roll_lanes(t, nx - 1) - roll_lanes(t, 1))
            above = roll_rows(wide, -1)[mine]
            below = roll_rows(wide, 1)[mine]
            if high == ny:
                above = jnp.where(row == CHUNK - 1, 0.0, above)
            if low == 0:
                below = jnp.where(row == 0, 0.0, below)
            totals[3] += weight * (above - below)
            moved = roll_lanes(t, k + 1)
            flux = roll_lanes(u * t, FLUX_LANE + k + 1)
            east = jnp.where(part == k, moved, jnp.where(part == FLUX_LANE + k, flux, east))
            west = jnp.where(part == k + 1, moved, jnp.where(part == FLUX_LANE + k + 1, flux, west))
            if start == 0:
                edge_rows[0, k : k + 1, :] = t[:1]
                edge_rows[0, pad + k : pad + k + 1, :] = v[:1] * t[:1]
            if start == ny - CHUNK:
                edge_rows[1, k : k + 1, :] = t[CHUNK - 1 :]
                edge_rows[1, pad + k : pad + k + 1, :] = v[CHUNK - 1 :] * t[CHUNK - 1 :]
        for ref, total in zip((sum_east, sum_north, force_east, force_north), totals):
            ref[inner] = total
        packs[0, inner], packs[1, inner] = east, west

    begin = 0
    for slab, count in zip(slabs, SLABS):
        for copy in slab:
            copy.wait()
        for start in range(0, ny, CHUNK):
            chunk(begin, count, start)
        begin += count
    for copy in bars:
        copy.wait()
    levels = levels_here[...]
    east = packs[0]
    west = roll_lanes(packs[1], nx - 1)
    own = jnp.where(lane < FLUX_LANE, east, roll_lanes(west, FLUX_LANE))
    packed[...] = own
    zonal = (
        force_east[...]
        - jnp.where(lane == nx - 1, column_sum(west, levels[:, nx - 1 :], 0), 0.0)
        + jnp.where(lane == 0, column_sum(east, levels[:, :1], 0), 0.0)
    )
    scale = TIMESTEP / depth
    slope = 0.5 * THERMAL_EXPANSION
    f = coriolis_of(shape, lax.axis_index("gy") * ny, total_rows)
    push_east = scale * (f * sum_north[...] - slope * zonal)
    push_north = scale * (-f * sum_east[...] - slope * force_north[...])
    force_east[...] = push_east
    force_north[...] = push_north
    fields = [bars_here[0], bars_here[1], bars_here[2], levels, push_east, push_north]
    low = lax.axis_index("ga") == 0
    even = lax.axis_index("gy") % 2 == 0
    for i, field in enumerate(fields):
        place = FIELD_LANE + W * i
        mine = (lane >= place) & (lane < place + W)
        west = jnp.where(mine, roll_lanes(field, place), west)
        east = jnp.where(mine, roll_lanes(field, place - (nx - W)), east)
        to_first[W * i : W * (i + 1), :] = jnp.where(even, field[ny - W :], field[:W])
        to_second[W * i : W * (i + 1), :] = jnp.where(even, field[:W], field[ny - W :])
    east = fold(east)
    west = fold(west)
    tall = ny - FOLD_ROWS
    first[:tall, :] = jnp.where(low, east, west)
    second[:tall, :] = jnp.where(low, west, east)
    small = lanes_of((8, nx))
    west = jnp.zeros((8, nx), jnp.float32)
    east = west
    for side in (0, 1):
        for group in range(pad // 8):
            place = pad * side + 8 * group
            mine = (small >= place) & (small < place + W)
            block = edge_rows[side, 8 * group : 8 * (group + 1), :]
            west = jnp.where(mine, roll_lanes(block, place), west)
            east = jnp.where(mine, roll_lanes(block, place - (nx - W)), east)
    first[tall:, :] = jnp.where(low, east, west)
    second[tall:, :] = jnp.where(low, west, east)
    start = 6 * W
    base = start + 2 * pad
    to_first[start:base, :] = jnp.where(even, edge_rows[1], edge_rows[0])
    to_second[start:base, :] = jnp.where(even, edge_rows[0], edge_rows[1])
    to_first[base:, :] = jnp.where(even, own[ny - 8 :], own[:8])
    to_second[base:, :] = jnp.where(even, own[:8], own[ny - 8 :])
    floor.wait()


def column_sum(values, levels, place):
    lane = lanes_of(values.shape)
    use = (lane >= place) & (lane < place + FLUX_LANE)
    weight = jnp.maximum(levels - (lane - place).astype(jnp.float32), 0.0)
    return jnp.sum(jnp.where(use, weight * values, 0.0), axis=1, keepdims=True)


def row_sum(values, levels):
    weight = jnp.maximum(levels - rows_of(values.shape).astype(jnp.float32), 0.0)
    return jnp.sum(weight * values, axis=0, keepdims=True)


def unfold_rows(east_block, west_block, side, pad):
    nx = east_block.shape[1]
    lane = lanes_of(east_block.shape)
    out = []
    for group in range(pad // 8):
        place = pad * side + 8 * group
        out.append(
            jnp.where(
                lane < W,
                roll_lanes(east_block, -place),
                jnp.where(lane >= nx - W, roll_lanes(west_block, nx - W - place), 0.0),
            )
        )
    return jnp.concatenate(out, axis=0)


def subcycles(fields, packed, from_west, from_east, from_south, from_north, own_north, own_south, pad):
    ny, nx = packed.shape
    p_row = 6 * W
    base = p_row + 2 * pad + 8
    tall = ny - FOLD_ROWS
    west = jnp.concatenate([from_south[base : base + 8], unfold(from_west[:tall]), from_north[base : base + 8]], axis=0)
    east = jnp.concatenate([from_south[base + 16 : base + 24], unfold(from_east[:tall]), from_north[base + 16 : base + 24]], axis=0)
    mine = jnp.concatenate([from_south[base - 8 : base], packed, from_north[base - 8 : base]], axis=0)
    lane = lanes_of(west.shape)
    row = rows_of(west.shape)
    centres = []
    halos = []
    for i, field in enumerate(fields):
        place = FIELD_LANE + W * i
        centres.append(jnp.concatenate([from_south[W * i : W * (i + 1)], field, from_north[W * i : W * (i + 1)]], axis=0))
        halos.append(
            jnp.where(
                lane < W,
                roll_lanes(east, -place),
                jnp.where(lane >= nx - W, roll_lanes(west, nx - W - place), 0.0),
            )
        )
    depth_centre, depth_halo = centres[3], halos[3]
    share = TIMESTEP / 20.0 * 0.5 * THERMAL_EXPANSION
    centres[4] = (
        centres[4]
        - jnp.where(lane == nx - 1, share * column_sum(east, depth_centre[:, nx - 1 :], 0), 0.0)
        + jnp.where(lane == 0, share * column_sum(west, depth_centre[:, :1], 0), 0.0)
    )
    halos[4] = (
        halos[4]
        + jnp.where(lane == 0, share * column_sum(mine, depth_halo[:, :1], 0), 0.0)
        - jnp.where(lane == nx - 1, share * column_sum(mine, depth_halo[:, nx - 1 :], FLUX_LANE), 0.0)
    )
    north_beyond = (
        from_north[p_row : p_row + pad],
        unfold_rows(from_north[base + 24 : base + 32], from_north[base + 8 : base + 16], 0, pad),
    )
    south_beyond = (
        from_south[p_row : p_row + pad],
        unfold_rows(from_south[base + 24 : base + 32], from_south[base + 8 : base + 16], 1, pad),
    )
    north_edge = (own_north, unfold_rows(from_east[tall:], from_west[tall:], 1, pad))
    south_edge = (own_south, unfold_rows(from_east[tall:], from_west[tall:], 0, pad))
    for part, fields, depths in ((0, centres, depth_centre), (1, halos, depth_halo)):
        top, bottom = W + ny - 1, W
        fields[5] = (
            fields[5]
            - jnp.where(row == top, share * row_sum(north_beyond[part], depths[top : top + 1]), 0.0)
            + jnp.where(row == bottom, share * row_sum(south_beyond[part], depths[bottom : bottom + 1]), 0.0)
            + jnp.where(row == top + 1, share * row_sum(north_edge[part], depths[top + 1 : top + 2]), 0.0)
            - jnp.where(row == bottom - 1, share * row_sum(south_edge[part], depths[bottom - 1 : bottom]), 0.0)
        )
    height, east_bar, north_bar, water, force_east, force_north = [
        jnp.concatenate([c, h], axis=1) for c, h in zip(centres, halos)
    ]
    wetness = jnp.where(water > 0.0, 1.0, 0.0)
    pull = (0.5 * SUBSTEP * GRAVITY / 20.0) * water
    push_east = SUBSTEP * wetness * force_east
    push_north = SUBSTEP * wetness * force_north
    spread = 0.5 * SUBSTEP * wetness
    cells, lines = height.shape[1], height.shape[0]
    for _ in range(NSUB):
        east_bar = wetness * east_bar + push_east - pull * (roll_lanes(height, cells - 1) - roll_lanes(height, 1))
        north_bar = wetness * north_bar + push_north - pull * (roll_rows(height, lines - 1) - roll_rows(height, 1))
        height = height - spread * (
            (roll_lanes(east_bar, cells - 1) - roll_lanes(east_bar, 1))
            + (roll_rows(north_bar, lines - 1) - roll_rows(north_bar, 1))
        )
    inner = slice(W, W + ny)
    return (
        height[inner, :nx],
        east_bar[inner, :nx],
        north_bar[inner, :nx],
        centres[4][inner],
        centres[5][inner],
    )


def ahead_less_behind(x):
    lane = lanes_of(x.shape)
    nx = x.shape[1]
    return jnp.where(lane == nx - 1, 0.0, roll_lanes(x, nx - 1)) - jnp.where(lane == 0, 0.0, roll_lanes(x, 1))


def above_less_below(x):
    row = rows_of(x.shape)
    ny = x.shape[0]
    return jnp.where(row == ny - 1, 0.0, roll_rows(x, ny - 1)) - jnp.where(row == 0, 0.0, roll_rows(x, 1))


def columns_kernel(
    total_rows,
    thermal,
    current,
    mixing,
    ground,
    velocity_east,
    velocity_north,
    mixed,
    ratios,
    inverses,
    lowers,
    planes,
    levels,
    thermal_here,
    current_here,
    mixing_here,
    sems,
):
    depth, ny, nx = thermal.shape
    shape = (ny, nx)
    step = depth // GROUPS
    floor = pltpu.make_async_copy(ground.at[0], levels, sems.at[0])
    floor.start()
    slabs = []
    for g in range(GROUPS):
        part = pl.ds(g * step, step)
        more = pl.ds(g * step, step + 1) if g == 0 else pl.ds(g * step + 1, min(step, depth - g * step - 1))
        slabs.append(
            [
                pltpu.make_async_copy(thermal.at[part], thermal_here.at[part], sems.at[1 + 3 * g]),
                pltpu.make_async_copy(current.at[:, part], current_here.at[:, part], sems.at[2 + 3 * g]),
                pltpu.make_async_copy(mixing.at[more], mixing_here.at[more], sems.at[3 + 3 * g]),
            ]
        )
        for copy in slabs[-1]:
            copy.start()
    zero = jnp.zeros(shape, jnp.float32)
    planes[0] = zero
    planes[1] = zero
    planes[2] = zero
    planes[3] = TIMESTEP * coriolis_of(shape, lax.axis_index("gy") * ny, total_rows)
    ratios[0] = zero
    mixed[0] = zero
    slope = 0.5 * TIMESTEP * THERMAL_EXPANSION
    floor.wait()

    def forward(k, carry):
        wet = levels[...]
        mask = wet > lax.convert_element_type(k, jnp.float32)
        raw = thermal_here[k]
        t = jnp.where(mask, raw, 0.0)
        u = current_here[0, k]
        v = current_here[1, k]
        dx = planes[0] + slope * ahead_less_behind(t)
        dy = planes[1] + slope * above_less_below(t)
        planes[0] = dx
        planes[1] = dy
        turn = planes[3]
        velocity_east[k] = u + turn * v - dx
        velocity_north[k] = v - turn * u - dy
        spread = ahead_less_behind(u * t) + above_less_below(v * t)
        source = jnp.where(mask, raw - 0.5 * TRANSPORT_SPEED * spread, 0.0)
        below = jnp.minimum(k + 1, depth - 1)
        upper = jnp.where(
            wet > lax.convert_element_type(k + 1, jnp.float32), 0.5 * MIXING * (mixing_here[k] + mixing_here[below]), 0.0
        )
        lower = planes[2]
        planes[2] = upper
        above = jnp.maximum(k - 1, 0)
        inverse = 1.0 / (1.0 + upper + lower * (1.0 + ratios[above]))
        lower = lower * inverse
        inverses[k] = inverse
        lowers[k] = lower
        ratios[k] = -upper * inverse
        mixed[k] = source * inverse + lower * mixed[above]
        return carry

    for g in range(GROUPS):
        for copy in slabs[g]:
            copy.wait()
        lax.fori_loop(g * step, (g + 1) * step, forward, 0, unroll=UNROLL)

    def backward(i, carry):
        k = depth - 2 - i
        mixed[k] = mixed[k] - ratios[k] * mixed[k + 1]
        return carry

    lax.fori_loop(0, depth - 1, backward, 0, unroll=BACK_UNROLL)


def zonal_kernel(levels, from_first, from_second, velocity, mixed, ratios, inverses, lowers, velocity_out, mixed_out, planes):
    depth, ny, nx = mixed.shape
    shape = (ny, nx)
    lane = lanes_of(shape)
    low = lax.axis_index("ga") == 0
    tall = ny - FOLD_ROWS
    from_east = unfold(jnp.where(low, from_first[:tall], from_second[:tall]))
    from_west = unfold(jnp.where(low, from_second[:tall], from_first[:tall]))
    spot = rows_of((nx, nx))
    place = lanes_of((nx, nx))
    spread_east = jnp.where((place == 2 * spot) & (spot < FIELD_LANE), 1.0, 0.0)
    spread_west = jnp.where((place == 2 * spot + 1) & (spot < FIELD_LANE), 1.0, 0.0)

    def spread(x, where):
        return jnp.dot(x, where, precision=lax.Precision.HIGHEST, preferred_element_type=jnp.float32)

    halo = spread(from_west, spread_west) - spread(from_east, spread_east)
    slope = 0.5 * TIMESTEP * THERMAL_EXPANSION
    planes[0] = jnp.where(lane < 2 * FLUX_LANE, slope, 0.5 * TRANSPORT_SPEED) * halo
    zero = jnp.zeros(shape, jnp.float32)
    planes[1] = zero
    mixed_out[0] = zero

    def forward(k, carry):
        edge = (lane == 0) | (lane == nx - 1)
        mask = edge & (levels[...] > lax.convert_element_type(k, jnp.float32))
        push = planes[1] + jnp.where(edge, roll_lanes(planes[0], nx - 1 - 2 * k), 0.0)
        planes[1] = push
        velocity_out[k] = velocity[k] + push
        source = jnp.where(mask, roll_lanes(planes[0], nx - 1 - 2 * FLUX_LANE - 2 * k), 0.0)
        above = jnp.maximum(k - 1, 0)
        mixed_out[k] = source * inverses[k] + lowers[k] * mixed_out[above]
        return carry

    lax.fori_loop(0, depth, forward, 0, unroll=UNROLL)

    def backward(i, later):
        k = depth - 1 - i
        now = mixed_out[k] - ratios[k] * planes[1]
        planes[1] = now
        mixed_out[k] = mixed[k] + now
        return later

    planes[1] = zero
    lax.fori_loop(0, depth, backward, 0, unroll=BACK_UNROLL)


def finish_kernel(
    levels,
    surface,
    transport,
    sum_east,
    sum_north,
    push_east,
    push_north,
    packed,
    own_first,
    own_second,
    zonal_first,
    zonal_second,
    merid_second,
    merid_first,
    velocity_east,
    velocity_north,
    mixed,
    ratios,
    inverses,
    lowers,
    mixed_out,
    velocity_out,
    height_out,
    transport_out,
    velocity,
    rims,
    shallow,
    sems,
):
    depth, ny, nx = mixed.shape
    pad = -(-depth // 8) * 8
    p_row, f_row = 6 * W, 6 * W + pad
    middle = pltpu.make_async_copy(mixed.at[:, pl.ds(8, ny - 16)], mixed_out.at[:, pl.ds(8, ny - 16)], sems.at[0])
    middle.start()
    low = lax.axis_index("ga") == 0
    even = lax.axis_index("gy") % 2 == 0

    def choose(test, a, b):
        return jnp.where(test, a[...], b[...]), jnp.where(test, b[...], a[...])

    from_east, from_west = choose(low, zonal_first, zonal_second)
    from_north, from_south = choose(even, merid_first, merid_second)
    own_north, own_south = choose(even, own_first.at[pl.ds(p_row, pad)], own_second.at[pl.ds(p_row, pad)])
    base = f_row + pad + 8
    swapped = []
    for block in (from_north, from_south):
        one, two = block[base : base + 16], block[base + 16 : base + 32]
        swapped.append(
            jnp.concatenate([block[:base], jnp.where(low, two, one), jnp.where(low, one, two)], axis=0)
        )
    from_north, from_south = swapped

    fields = [surface[...], transport[0], transport[1], levels[...], push_east[...], push_north[...]]
    height, east_bar, north_bar, force_east, force_north = subcycles(
        fields, packed[...], from_west, from_east, from_south, from_north, own_north, own_south, pad
    )
    shallow[0] = height
    shallow[1] = east_bar
    shallow[2] = north_bar
    flat = [
        pltpu.make_async_copy(shallow.at[0], height_out, sems.at[3]),
        pltpu.make_async_copy(shallow.at[pl.ds(1, 2)], transport_out, sems.at[4]),
    ]
    for copy in flat:
        copy.start()
    count = jnp.maximum(levels[...], 1.0)
    shallow[3] = east_bar - (sum_east[...] + depth * force_east) / count
    shallow[4] = north_bar - (sum_north[...] + depth * force_north) / count

    row = rows_of((8, nx))
    places = (0, ny - 8)
    parts = (row == 0, row == 7)
    signs = (1.0, -1.0)
    blocks = (from_south, from_north)
    slope = 0.5 * TIMESTEP * THERMAL_EXPANSION
    carried = [jnp.zeros((8, nx), jnp.float32) for _ in range(4)]
    wet = levels[...]
    step = depth // GROUPS
    slabs = []
    for k in range(depth):
        mask = wet > float(k)
        velocity[0, k] = jnp.where(mask, velocity_east[k] + shallow[3], 0.0)
        velocity[1, k, 8 : ny - 8] = jnp.where(
            mask[8 : ny - 8], velocity_north[k, 8 : ny - 8] + shallow[4, 8 : ny - 8], 0.0
        )
        for s in (0, 1):
            place = pl.ds(places[s], 8)
            carried[s] += jnp.where(parts[s], signs[s] * slope * blocks[s][p_row + k : p_row + k + 1], 0.0)
            velocity[1, k, place] = jnp.where(
                mask[places[s] : places[s] + 8], velocity_north[k, place] + carried[s] + shallow[4, place], 0.0
            )
        if (k + 1) % step == 0:
            part = pl.ds(k + 1 - step, step)
            copy = pltpu.make_async_copy(velocity.at[:, part], velocity_out.at[:, part], sems.at[5 + k // step])
            copy.start()
            slabs.append(copy)
    solved = [[], []]
    for k in range(depth):
        for s in (0, 1):
            place = pl.ds(places[s], 8)
            mask = parts[s] & (wet[places[s] : places[s] + 8] > float(k))
            flux = blocks[s][f_row + k : f_row + k + 1]
            source = jnp.where(mask, signs[s] * 0.5 * TRANSPORT_SPEED * flux, 0.0)
            carried[2 + s] = source * inverses[k, place] + lowers[k, place] * carried[2 + s]
            solved[s].append(carried[2 + s])
    for s in (0, 1):
        place = pl.ds(places[s], 8)
        later = jnp.zeros((8, nx), jnp.float32)
        for k in range(depth - 1, -1, -1):
            later = solved[s][k] - ratios[k, place] * later
            rims[k, pl.ds(8 * s, 8)] = mixed[k, place] + later
    edges = [
        pltpu.make_async_copy(rims.at[:, pl.ds(0, 8)], mixed_out.at[:, pl.ds(0, 8)], sems.at[1]),
        pltpu.make_async_copy(rims.at[:, pl.ds(8, 8)], mixed_out.at[:, pl.ds(ny - 8, 8)], sems.at[2]),
    ]
    for copy in edges:
        copy.start()
    for copy in [middle] + edges + flat + slabs:
        copy.wait()


def partner(block, zonal, parity):
    sx, sy, sa = (lax.axis_size(a) for a in AXES)
    count = sx * sa
    pairs = []
    for x in range(count):
        for y in range(sy):
            tx, ty = x, y
            if zonal:
                tx = (x + 1 if x % 2 == parity else x - 1) % count
            else:
                ty = y + 1 if y % 2 == parity else y - 1
            if 0 <= ty < sy:
                source = (x // sa * sy + y) * sa + x % sa
                pairs.append((source, (tx // sa * sy + ty) * sa + tx % sa))
    return lax.ppermute(block, AXES, pairs)


def estimate(flops, moved):
    return pl.CostEstimate(flops=flops, bytes_accessed=moved, transcendentals=0)


def per_device(thermal, current, mixing, surface, transport, flag, wet):
    depth, ny, nx = thermal.shape
    total_rows = ny * lax.axis_size("gy")
    pad = -(-depth // 8) * 8
    f32 = jnp.float32
    here = pl.BlockSpec(memory_space=pltpu.VMEM)
    far = pl.BlockSpec(memory_space=pltpu.HBM)
    params = pltpu.CompilerParams(vmem_limit_bytes=VMEM_BYTES)
    rows = 6 * W + 2 * pad + 8
    sd = jax.ShapeDtypeStruct
    cube = sd((depth, ny, nx), f32)
    pair = sd((2, depth, ny, nx), f32)
    cells = depth * ny * nx
    plane = sd((ny, nx), f32)
    edge = sd((ny - FOLD_ROWS + 8, nx), f32)
    outs = pl.pallas_call(
        functools.partial(edges_kernel, total_rows),
        out_shape=[edge, edge, sd((rows, nx), f32), sd((rows, nx), f32)] + [plane] * 6 + [sd((24, ny, nx), f32)],
        in_specs=[far] * 6,
        out_specs=[here] * 10 + [far],
        scratch_shapes=[
            pltpu.VMEM((depth, ny, nx), f32),
            pltpu.VMEM((2, depth, ny, nx), f32),
            pltpu.VMEM((3, ny, nx), f32),
            pltpu.VMEM((2, 2 * pad, nx), f32),
            pltpu.VMEM((2, ny, nx), f32),
            pltpu.VMEM((ny, nx), jnp.int32),
            pltpu.VMEM((ny, nx), jnp.int32),
            pltpu.SemaphoreType.DMA((5 + 3 * GROUPS,)),
        ],
        compiler_params=pltpu.CompilerParams(vmem_limit_bytes=EDGES_VMEM),
        cost_estimate=estimate(30 * cells, 12 * cells),
        name="edges",
    )(thermal, current, surface, transport, flag, wet)
    first, second, to_first, to_second, packed, levels, sum_east, sum_north, force_east, force_north, ground = outs
    zonal_first = partner(first, True, 0)
    zonal_second = partner(second, True, 1)
    velocity_east, velocity_north, mixed, ratios, inverses, lowers = pl.pallas_call(
        functools.partial(columns_kernel, total_rows),
        out_shape=[cube] * 6,
        in_specs=[far] * 4,
        out_specs=[here] * 6,
        scratch_shapes=[
            pltpu.VMEM((4, ny, nx), f32),
            pltpu.VMEM((ny, nx), f32),
            pltpu.VMEM((depth, ny, nx), f32),
            pltpu.VMEM((2, depth, ny, nx), f32),
            pltpu.VMEM((depth, ny, nx), f32),
            pltpu.SemaphoreType.DMA((1 + 3 * GROUPS,)),
        ],
        compiler_params=pltpu.CompilerParams(vmem_limit_bytes=COLUMNS_VMEM),
        cost_estimate=estimate(100 * cells, 40 * cells),
        name="columns",
    )(thermal, current, mixing, ground)
    zonal_first, zonal_second, velocity_east = lax.optimization_barrier((zonal_first, zonal_second, velocity_east))
    even = lax.axis_index("gy") % 2 == 0
    tall = ny - FOLD_ROWS
    top = [zonal_first[tall - 8 :], zonal_second[tall - 8 :]]
    bottom = [zonal_first[:8], zonal_first[tall:], zonal_second[:8], zonal_second[tall:]]
    top = jnp.concatenate(top, axis=0)
    bottom = jnp.concatenate(bottom, axis=0)
    merid_first = partner(jnp.concatenate([to_first, jnp.where(even, top, bottom)], axis=0), False, 0)
    merid_second = partner(jnp.concatenate([to_second, jnp.where(even, bottom, top)], axis=0), False, 1)
    velocity_east, mixed = pl.pallas_call(
        zonal_kernel,
        out_shape=[cube, cube],
        in_specs=[here] * 8,
        out_specs=[here] * 2,
        scratch_shapes=[pltpu.VMEM((2, ny, nx), f32)],
        compiler_params=params,
        cost_estimate=estimate(20 * cells, 20 * cells),
        name="zonal",
    )(levels, zonal_first, zonal_second, velocity_east, mixed, ratios, inverses, lowers)
    return pl.pallas_call(
        finish_kernel,
        out_shape=[cube, pair, sd((ny, nx), f32), sd((2, ny, nx), f32)],
        in_specs=[here] * 20,
        out_specs=[far] * 4,
        scratch_shapes=[
            pltpu.VMEM((2, depth, ny, nx), f32),
            pltpu.VMEM((depth, 16, nx), f32),
            pltpu.VMEM((5, ny, nx), f32),
            pltpu.SemaphoreType.DMA((5 + GROUPS,)),
        ],
        compiler_params=params,
        name="finish",
    )(
        levels,
        surface,
        transport,
        sum_east,
        sum_north,
        force_east,
        force_north,
        packed,
        to_first,
        to_second,
        zonal_first,
        zonal_second,
        merid_second,
        merid_first,
        velocity_east,
        velocity_north,
        mixed,
        ratios,
        inverses,
        lowers,
    )


def solution(mesh):
    placed = (
        P(None, "gy", ("gx", "ga")),
        P(None, None, "gy", ("gx", "ga")),
        P(None, "gy", ("gx", "ga")),
        P("gy", ("gx", "ga")),
        P(None, "gy", ("gx", "ga")),
        P("gy", ("gx", "ga")),
        P("gy", ("gx", "ga")),
    )
    return jax.shard_map(
        per_device,
        mesh=mesh,
        in_specs=placed,
        out_specs=(
            P(None, "gy", ("gx", "ga")),
            P(None, None, "gy", ("gx", "ga")),
            P("gy", ("gx", "ga")),
            P(None, "gy", ("gx", "ga")),
        ),
        check_vma=False,
    )
```

profile of v0, /device:TPU:1, one launch (start us, length us, event | category | flops | bytes accessed | tf_op | source)
XLA Modules:
  0.0 29.3 jit_solution(4545498584927440337)
XLA Ops:
  0.6 3.6 %edges.1 = (f32[104,128]{1,0:T(8,128)S(1)}, f32[104,128]{1,0:T(8,128)S(1)}, f32[104,128]{1,0:T(8,128)S(1)}, f32[104,128]{1,0:T(8,128)S(1)}, f32[128,128]{1,0:T(8...) custom-call(f32[20,128,128]{2,1,0:T(8,128)} %thermal.3, ...), custom_call_target="tpu_custom_call" | custom-call | flops 9830400 | bytes 3932160 | tf_op jit(solution)/shard_map/edges/pallas_call | solution.py:665
  4.3 7.8 %collective-permute-start = (f32[104,128]{1,0:T(8,128)S(1)}, f32[104,128]{1,0:T(8,128)S(1)}, u32[]{:S(2)}, u32[]{:S(2)}) collective-permute-start(f32[104,128]{1,0:T(8,128)S(1)} %get-tuple-element.34), channel_id=1, source_target_pairs={{0,1},{2,3},{4,5},{6,7},{8,9},{10,11},{12,13},{14,15},{1,0},{3,2},... | collective-permute-start | bytes 159752 | tf_op jit(solution)/shard_map/ppermute | solution.py:643
  12.1 2.3 %collective-permute-start.1 = (f32[104,128]{1,0:T(8,128)S(1)}, f32[104,128]{1,0:T(8,128)S(1)}, u32[]{:S(2)}, u32[]{:S(2)}) collective-permute-start(f32[104,128]{1,0:T(8,128)S(1)} %get-tuple-element.35), channel_id=1, source_target_pairs={{0,241},{2,243},{4,245},{6,247},{8,249},{10,251},{12,253},{14,255}... | collective-permute-start | bytes 159752 | tf_op jit(solution)/shard_map/ppermute | solution.py:643
  14.4 4.2 %columns.1 = (f32[20,128,128]{2,1,0:T(8,128)S(1)}, f32[20,128,128]{2,1,0:T(8,128)S(1)}, f32[20,128,128]{2,1,0:T(8,128)S(1)}, f32[20,128,128]{2,1,0:T(8,128)S(1)}...) custom-call(f32[20,128,128]{2,1,0:T(8,128)} %thermal.3, f32[2,20,128,128]{3,2,1,0:T(8,128)} %current.3, ...), custom_call_target="tpu_custom_call" | custom-call | flops 32768000 | bytes 13107200 | tf_op jit(solution)/shard_map/columns/pallas_call | solution.py:687
  18.5 0.0 collective-permute-done.from_first.zonal_first
  18.5 0.0 collective-permute-done.1.from_second.zonal_second
  18.6 4.9 %collective-permute-start.2 = (f32[136,128]{1,0:T(8,128)S(1)}, f32[136,128]{1,0:T(8,128)S(1)}, u32[]{:S(2)}, u32[]{:S(2)}) collective-permute-start(f32[136,128]{1,0:T(8,128)S(1)} %pad_maximum_fusion), channel_id=1, source_target_pairs={{2,4},{4,2},{6,8},{8,6},{10,12},{12,10},{3,5},{5,3},{7,9},{9,7},{1... | collective-permute-start | bytes 208904 | tf_op jit(solution)/shard_map/ppermute | solution.py:643
  23.6 0.1 collective-permute-start.3
  23.7 0.0 copy-start
  23.7 0.0 copy-start.1
  23.7 1.6 %zonal.1 = (f32[20,128,128]{2,1,0:T(8,128)S(1)}, f32[20,128,128]{2,1,0:T(8,128)S(1)}) custom-call(f32[128,128]{1,0:T(8,128)S(1)} %get-tuple-element.26.levels, f32[104,128]{1,0:T(8,128)S(1)} %collective-permute-done.from_first.zonal_first, f32[104,128]{1,0:T(8,128)S(1)} %collective-permute-done.1.from_second.zonal_second, ...), custom_call_target="tpu_custom_call" | custom-call | flops 6553600 | bytes 6553600 | tf_op jit(solution)/shard_map/zonal/pallas_call | solution.py:713
  25.3 0.2 collective-permute-done.2.merid_second
  25.5 0.0 collective-permute-done.3.merid_first
  25.5 0.0 copy-done
  25.5 0.0 copy-done.1
  25.5 3.7 %finish.1 = (f32[20,128,128]{2,1,0:T(8,128)}, f32[2,20,128,128]{3,2,1,0:T(8,128)}, f32[128,128]{1,0:T(8,128)}, f32[2,128,128]{2,1,0:T(8,128)}) custom-call(f32[128,128]{1,0:T(8,128)S(1)} %get-tuple-element.26.levels, f32[128,128]{1,0:T(8,128)S(1)} %copy-done.1, f32[2,128,128]{2,1,0:T(8,128)S(1)} %copy-done, f32[128,128]{1,0:T(8,128)S(1)} %get-tuple-element.27.sum_east, ...), custom_call_target="tpu_custom_call" | custom-call | tf_op jit(solution)/shard_map/finish/pallas_call | solution.py:723
  (6 shorter events, 0.0 us)
Async XLA Ops:
  4.3 14.3 %collective-permute-start = (f32[104,128]{1,0:T(8,128)S(1)}, f32[104,128]{1,0:T(8,128)S(1)}, u32[]{:S(2)}, u32[]{:S(2)}) collective-permute-start(f32[104,128]{1,0:T(8,128)S(1)} %get-tuple-element.34), channel_id=1, source_target_pairs={{0,1},{2,3},{4,5},{6,7},{8,9},{10,11},{12,13},{14,15},{1,0},{3,2},... | collective-permute-start | bytes 159752 | tf_op jit(solution)/shard_map/ppermute | solution.py:643
  12.1 6.5 %collective-permute-start.1 = (f32[104,128]{1,0:T(8,128)S(1)}, f32[104,128]{1,0:T(8,128)S(1)}, u32[]{:S(2)}, u32[]{:S(2)}) collective-permute-start(f32[104,128]{1,0:T(8,128)S(1)} %get-tuple-element.35), channel_id=1, source_target_pairs={{0,241},{2,243},{4,245},{6,247},{8,249},{10,251},{12,253},{14,255}... | collective-permute-start | bytes 159752 | tf_op jit(solution)/shard_map/ppermute | solution.py:643
  18.6 6.9 %collective-permute-start.2 = (f32[136,128]{1,0:T(8,128)S(1)}, f32[136,128]{1,0:T(8,128)S(1)}, u32[]{:S(2)}, u32[]{:S(2)}) collective-permute-start(f32[136,128]{1,0:T(8,128)S(1)} %pad_maximum_fusion), channel_id=1, source_target_pairs={{2,4},{4,2},{6,8},{8,6},{10,12},{12,10},{3,5},{5,3},{7,9},{9,7},{1... | collective-permute-start | bytes 208904 | tf_op jit(solution)/shard_map/ppermute | solution.py:643
  23.6 2.0 %collective-permute-start.3 = (f32[136,128]{1,0:T(8,128)S(1)}, f32[136,128]{1,0:T(8,128)S(1)}, u32[]{:S(2)}, u32[]{:S(2)}) collective-permute-start(f32[136,128]{1,0:T(8,128)S(1)} %pad_maximum_fusion.1), channel_id=1, source_target_pairs={{0,2},{2,0},{4,6},{6,4},{8,10},{10,8},{12,14},{14,12},{1,3},{3,1},... | collective-permute-start | bytes 208904 | tf_op jit(solution)/shard_map/ppermute | solution.py:643
  23.7 1.9 %copy-start = (f32[2,128,128]{2,1,0:T(8,128)S(1)}, f32[2,128,128]{2,1,0:T(8,128)}, u32[]{:S(2)}) copy-start(f32[2,128,128]{2,1,0:T(8,128)} %transport.3) | copy-start | bytes 393220
  23.7 1.9 %copy-start.1 = (f32[128,128]{1,0:T(8,128)S(1)}, f32[128,128]{1,0:T(8,128)}, u32[]{:S(2)}) copy-start(f32[128,128]{1,0:T(8,128)} %surface.3) | copy-start | bytes 196612
where the time goes:
time: 29.4 us; the launch traced here: 29.3 us
  starting transfers between devices  15.1 us (51%)
  Pallas kernels  13.1 us (45%)
  between operations  0.76 us (3%)
    ppermute x4, starting transfers between devices, partner(): return lax.ppermute(block, AXES, pairs)  15.1 us
    pallas_call x1, Pallas kernels, per_device(): pl.pallas_call(functools.partial(columns_kernel, total_rows), out_shape=[...  4.16 us
    pallas_call x1, Pallas kernels, per_device(): pl.pallas_call(finish_kernel, out_shape=[cube, pair, sd((ny, nx), f32), s...  3.75 us
    pallas_call x1, Pallas kernels, per_device(): pl.pallas_call(functools.partial(edges_kernel, total_rows), out_shape=[ed...  3.62 us
    pallas_call x1, Pallas kernels, per_device(): pl.pallas_call(zonal_kernel, out_shape=[cube, cube], in_specs=[here] * 8,...  1.59 us
  transfers between devices with their start and end apart: 4, of which 1 were waited for; matrix products, arithmetic and copies ran while one was open for 0% of the time, Pallas kernels for 20%

commit v1 on v0

--- a/solution.py
+++ b/solution.py
@@ -20,11 +20,13 @@
 FIELDS = 6
 FLUX_LANE = 20
 FIELD_LANE = 40
-FOLD_LANE = 88
-FOLD = 30
-FOLD_ROWS = 32
+WIDTHS = (7, 7, 6, 6, 5, 4)
+FREE_LANE = 75
+EDGE_ROWS = 80
+WIDE = 53
+PIECES = tuple(((1 + i, FREE_LANE), (t, p)) for i, (t, p) in enumerate(((7, 75), (7, 97), (8, 75), (8, 97), (0, 99), (9, 99))))
 GROUPS = 4
-CHUNK = 32
+CHUNK = 16
 SLABS = (4, 6, 6, 4)
 UNROLL = 5
 BACK_UNROLL = 4
@@ -55,28 +57,36 @@
     return 0.3 + 0.4 * rows / total_rows
 
 
-def fold(full):
+def fold(full, edges):
     ny, nx = full.shape
-    lane = lanes_of((FOLD_ROWS, nx))
-    low = (ny - FOLD_ROWS) // 2
-    middle = full[low : low + FOLD_ROWS]
-    rest = jnp.concatenate([full[:low], full[low + FOLD_ROWS :]], axis=0)
-    out = []
-    for piece in range(3):
-        part = rest[FOLD_ROWS * piece : FOLD_ROWS * (piece + 1)]
-        out.append(jnp.where(lane < FOLD_LANE, part, roll_lanes(middle, FOLD_LANE - FOLD * piece)))
-    return jnp.concatenate(out, axis=0)
+    lane = lanes_of((8, nx))
+    half = EDGE_ROWS // 2
+    tiles = [full[8 * i : 8 * i + 8] for i in range(half // 8)]
+    tiles += [full[ny - half + 8 * i : ny - half + 8 * i + 8] for i in range(half // 8)]
+    pad = edges[0].shape[0]
+    for tile, block, shift_by in ((0, edges[0], edges[2]), (len(tiles) - 1, edges[1], edges[2])):
+        for group in range(pad // 8):
+            place = FREE_LANE + 8 * group
+            mine = (lane >= place) & (lane < place + 8)
+            tiles[tile] = jnp.where(mine, roll_lanes(block[8 * group : 8 * group + 8], place - shift_by), tiles[tile])
+    for i, ((wide, place), (narrow, spot)) in enumerate(PIECES):
+        middle = full[half + 8 * i : half + 8 * i + 8]
+        tiles[wide] = jnp.where(lane >= place, roll_lanes(middle, place), tiles[wide])
+        mine = (lane >= spot) & (lane < spot + FREE_LANE - WIDE)
+        tiles[narrow] = jnp.where(mine, roll_lanes(middle, spot - WIDE), tiles[narrow])
+    return jnp.concatenate(tiles, axis=0)
 
 
 def unfold(folded):
-    rows, nx = folded.shape
-    lane = lanes_of((FOLD_ROWS, nx))
-    middle = jnp.zeros((FOLD_ROWS, nx), jnp.float32)
-    for piece in range(3):
-        part = folded[FOLD_ROWS * piece : FOLD_ROWS * (piece + 1)]
-        mine = (lane >= FOLD * piece) & (lane < FOLD * (piece + 1))
-        middle = jnp.where(mine, roll_lanes(part, FOLD * piece - FOLD_LANE), middle)
-    return jnp.concatenate([folded[: rows // 2], middle, folded[rows // 2 :]], axis=0)
+    nx = folded.shape[1]
+    lane = lanes_of((8, nx))
+    tiles = []
+    for (wide, place), (narrow, spot) in PIECES:
+        one = roll_lanes(folded[8 * wide : 8 * wide + 8], -place)
+        two = roll_lanes(folded[8 * narrow : 8 * narrow + 8], WIDE - spot)
+        tiles.append(jnp.where(lane < WIDE, one, two))
+    half = EDGE_ROWS // 2
+    return jnp.concatenate([folded[:half], *tiles, folded[half:]], axis=0)
 
 
 def edges_kernel(
@@ -163,7 +173,9 @@
             v = current_here[1, k, inner]
             totals[0] += jnp.where(mask, u, 0.0)
             totals[1] += jnp.where(mask, v, 0.0)
-            totals[2] += weight * (roll_lanes(t, nx - 1) - roll_lanes(t, 1))
+            ahead = jnp.where(part == nx - 1, 0.0, roll_lanes(t, nx - 1))
+            behind = jnp.where(part == 0, 0.0, roll_lanes(t, 1))
+            totals[2] += weight * (ahead - behind)
             above = roll_rows(wide, -1)[mine]
             below = roll_rows(wide, 1)[mine]
             if high == ny:
@@ -199,45 +211,36 @@
     west = roll_lanes(packs[1], nx - 1)
     own = jnp.where(lane < FLUX_LANE, east, roll_lanes(west, FLUX_LANE))
     packed[...] = own
-    zonal = (
-        force_east[...]
-        - jnp.where(lane == nx - 1, column_sum(west, levels[:, nx - 1 :], 0), 0.0)
-        + jnp.where(lane == 0, column_sum(east, levels[:, :1], 0), 0.0)
-    )
     scale = TIMESTEP / depth
     slope = 0.5 * THERMAL_EXPANSION
     f = coriolis_of(shape, lax.axis_index("gy") * ny, total_rows)
-    push_east = scale * (f * sum_north[...] - slope * zonal)
+    push_east = scale * (f * sum_north[...] - slope * force_east[...])
     push_north = scale * (-f * sum_east[...] - slope * force_north[...])
     force_east[...] = push_east
     force_north[...] = push_north
-    fields = [bars_here[0], bars_here[1], bars_here[2], levels, push_east, push_north]
     low = lax.axis_index("ga") == 0
     even = lax.axis_index("gy") % 2 == 0
-    for i, field in enumerate(fields):
-        place = FIELD_LANE + W * i
-        mine = (lane >= place) & (lane < place + W)
-        west = jnp.where(mine, roll_lanes(field, place), west)
-        east = jnp.where(mine, roll_lanes(field, place - (nx - W)), east)
+    for i, field in enumerate([bars_here[0], bars_here[1], bars_here[2], levels, push_east, push_north]):
         to_first[W * i : W * (i + 1), :] = jnp.where(even, field[ny - W :], field[:W])
         to_second[W * i : W * (i + 1), :] = jnp.where(even, field[:W], field[ny - W :])
-    east = fold(east)
-    west = fold(west)
-    tall = ny - FOLD_ROWS
-    first[:tall, :] = jnp.where(low, east, west)
-    second[:tall, :] = jnp.where(low, west, east)
-    small = lanes_of((8, nx))
-    west = jnp.zeros((8, nx), jnp.float32)
-    east = west
-    for side in (0, 1):
-        for group in range(pad // 8):
-            place = pad * side + 8 * group
-            mine = (small >= place) & (small < place + W)
-            block = edge_rows[side, 8 * group : 8 * (group + 1), :]
-            west = jnp.where(mine, roll_lanes(block, place), west)
-            east = jnp.where(mine, roll_lanes(block, place - (nx - W)), east)
-    first[tall:, :] = jnp.where(low, east, west)
-    second[tall:, :] = jnp.where(low, west, east)
+    height = bars_here[0]
+    east_bar = bars_here[1] + SUBSTEP * push_east
+    north_bar = bars_here[2] + SUBSTEP * push_north
+    pull = (0.5 * SUBSTEP * GRAVITY / depth) * levels
+    east_next = jnp.where(levels > 0.0, east_bar, 0.0) - pull * (roll_lanes(height, nx - 1) - roll_lanes(height, 1))
+    last = WIDTHS[1] - 1
+    east_bar = jnp.where((lane == last) | (lane == nx - 1 - last), east_next, east_bar)
+    place = FIELD_LANE
+    for field, width in zip([height, east_bar, north_bar, levels, push_east, push_north], WIDTHS):
+        mine = (lane >= place) & (lane < place + width)
+        west = jnp.where(mine, roll_lanes(field, place), west)
+        east = jnp.where(mine, roll_lanes(field, place - (nx - width)), east)
+        place += width
+    rims = [edge_rows[0, :pad], edge_rows[1, :pad]]
+    east = fold(east, [*rims, nx - W])
+    west = fold(west, [*rims, 0])
+    first[...] = jnp.where(low, east, west)
+    second[...] = jnp.where(low, west, east)
     start = 6 * W
     base = start + 2 * pad
     to_first[start:base, :] = jnp.where(even, edge_rows[1], edge_rows[0])
@@ -247,11 +250,23 @@
     floor.wait()
 
 
-def column_sum(values, levels, place):
+def edge_matrices(nx):
+    row = rows_of((nx, nx))
+    lane = lanes_of((nx, nx))
+    first = lane < FLUX_LANE
+    second = (lane >= FLUX_LANE) & (lane < 2 * FLUX_LANE)
+    copy = jnp.where((first & (row == 0)) | (second & (row == nx - 1)), 1.0, 0.0)
+    first = (row < FLUX_LANE) & (lane == 0)
+    second = (row >= FLUX_LANE) & (row < 2 * FLUX_LANE) & (lane == nx - 1)
+    return copy, jnp.where(first, 1.0, jnp.where(second, -1.0, 0.0))
+
+
+def across_edges(values, levels, copy, add):
     lane = lanes_of(values.shape)
-    use = (lane >= place) & (lane < place + FLUX_LANE)
-    weight = jnp.maximum(levels - (lane - place).astype(jnp.float32), 0.0)
-    return jnp.sum(jnp.where(use, weight * values, 0.0), axis=1, keepdims=True)
+    levels = jnp.dot(levels, copy, preferred_element_type=jnp.float32)
+    weight = jnp.maximum(levels - jnp.where(lane < FLUX_LANE, lane, lane - FLUX_LANE).astype(jnp.float32), 0.0)
+    terms = jnp.where(lane < 2 * FLUX_LANE, weight * values, 0.0)
+    return jnp.dot(terms, add, precision=lax.Precision.HIGHEST, preferred_element_type=jnp.float32)
 
 
 def row_sum(values, levels):
@@ -259,12 +274,12 @@
     return jnp.sum(weight * values, axis=0, keepdims=True)
 
 
-def unfold_rows(east_block, west_block, side, pad):
+def unfold_rows(east_block, west_block, pad):
     nx = east_block.shape[1]
     lane = lanes_of(east_block.shape)
     out = []
     for group in range(pad // 8):
-        place = pad * side + 8 * group
+        place = FREE_LANE + 8 * group
         out.append(
             jnp.where(
                 lane < W,
@@ -275,83 +290,105 @@
     return jnp.concatenate(out, axis=0)
 
 
-def subcycles(fields, packed, from_west, from_east, from_south, from_north, own_north, own_south, pad):
+def subcycles(tank, fields, packed, from_west, from_east, from_south, from_north, own_north, own_south, pad):
     ny, nx = packed.shape
     p_row = 6 * W
     base = p_row + 2 * pad + 8
-    tall = ny - FOLD_ROWS
-    west = jnp.concatenate([from_south[base : base + 8], unfold(from_west[:tall]), from_north[base : base + 8]], axis=0)
-    east = jnp.concatenate([from_south[base + 16 : base + 24], unfold(from_east[:tall]), from_north[base + 16 : base + 24]], axis=0)
+    west = jnp.concatenate([from_south[base : base + 8], unfold(from_west), from_north[base : base + 8]], axis=0)
+    east = jnp.concatenate([from_south[base + 8 : base + 16], unfold(from_east), from_north[base + 8 : base + 16]], axis=0)
     mine = jnp.concatenate([from_south[base - 8 : base], packed, from_north[base - 8 : base]], axis=0)
     lane = lanes_of(west.shape)
     row = rows_of(west.shape)
     centres = []
     halos = []
-    for i, field in enumerate(fields):
-        place = FIELD_LANE + W * i
+    place = FIELD_LANE
+    for i, (field, width) in enumerate(zip(fields, WIDTHS)):
         centres.append(jnp.concatenate([from_south[W * i : W * (i + 1)], field, from_north[W * i : W * (i + 1)]], axis=0))
         halos.append(
             jnp.where(
-                lane < W,
+                lane < width,
                 roll_lanes(east, -place),
-                jnp.where(lane >= nx - W, roll_lanes(west, nx - W - place), 0.0),
+                jnp.where(lane >= nx - width, roll_lanes(west, nx - width - place), 0.0),
             )
         )
+        place += width
     depth_centre, depth_halo = centres[3], halos[3]
     share = TIMESTEP / 20.0 * 0.5 * THERMAL_EXPANSION
-    centres[4] = (
-        centres[4]
-        - jnp.where(lane == nx - 1, share * column_sum(east, depth_centre[:, nx - 1 :], 0), 0.0)
-        + jnp.where(lane == 0, share * column_sum(west, depth_centre[:, :1], 0), 0.0)
-    )
-    halos[4] = (
-        halos[4]
-        + jnp.where(lane == 0, share * column_sum(mine, depth_halo[:, :1], 0), 0.0)
-        - jnp.where(lane == nx - 1, share * column_sum(mine, depth_halo[:, nx - 1 :], FLUX_LANE), 0.0)
-    )
+    copy, add = edge_matrices(nx)
+    beyond = jnp.where(lane < FLUX_LANE, west, roll_lanes(east, FLUX_LANE))
+    centres[4] = centres[4] + share * across_edges(beyond, depth_centre, copy, add)
+    lacking = share * across_edges(mine, depth_halo, copy, add)
+    halos[4] = halos[4] + lacking
+    halos[1] = halos[1] + SUBSTEP * lacking
     north_beyond = (
         from_north[p_row : p_row + pad],
-        unfold_rows(from_north[base + 24 : base + 32], from_north[base + 8 : base + 16], 0, pad),
+        unfold_rows(from_north[base + 8 : base + 16], from_north[base : base + 8], pad),
     )
     south_beyond = (
         from_south[p_row : p_row + pad],
-        unfold_rows(from_south[base + 24 : base + 32], from_south[base + 8 : base + 16], 1, pad),
+        unfold_rows(from_south[base + 8 : base + 16], from_south[base : base + 8], pad),
     )
-    north_edge = (own_north, unfold_rows(from_east[tall:], from_west[tall:], 1, pad))
-    south_edge = (own_south, unfold_rows(from_east[tall:], from_west[tall:], 0, pad))
+    end = EDGE_ROWS - 8
+    north_edge = (own_north, unfold_rows(from_east[end:], from_west[end:], pad))
+    south_edge = (own_south, unfold_rows(from_east[:8], from_west[:8], pad))
     for part, fields, depths in ((0, centres, depth_centre), (1, halos, depth_halo)):
         top, bottom = W + ny - 1, W
-        fields[5] = (
-            fields[5]
+        lacking = (
+            jnp.where(row == bottom, share * row_sum(south_beyond[part], depths[bottom : bottom + 1]), 0.0)
             - jnp.where(row == top, share * row_sum(north_beyond[part], depths[top : top + 1]), 0.0)
-            + jnp.where(row == bottom, share * row_sum(south_beyond[part], depths[bottom : bottom + 1]), 0.0)
             + jnp.where(row == top + 1, share * row_sum(north_edge[part], depths[top + 1 : top + 2]), 0.0)
             - jnp.where(row == bottom - 1, share * row_sum(south_edge[part], depths[bottom - 1 : bottom]), 0.0)
         )
-    height, east_bar, north_bar, water, force_east, force_north = [
-        jnp.concatenate([c, h], axis=1) for c, h in zip(centres, halos)
-    ]
-    wetness = jnp.where(water > 0.0, 1.0, 0.0)
-    pull = (0.5 * SUBSTEP * GRAVITY / 20.0) * water
-    push_east = SUBSTEP * wetness * force_east
-    push_north = SUBSTEP * wetness * force_north
-    spread = 0.5 * SUBSTEP * wetness
-    cells, lines = height.shape[1], height.shape[0]
-    for _ in range(NSUB):
-        east_bar = wetness * east_bar + push_east - pull * (roll_lanes(height, cells - 1) - roll_lanes(height, 1))
-        north_bar = wetness * north_bar + push_north - pull * (roll_rows(height, lines - 1) - roll_rows(height, 1))
-        height = height - spread * (
-            (roll_lanes(east_bar, cells - 1) - roll_lanes(east_bar, 1))
-            + (roll_rows(north_bar, lines - 1) - roll_rows(north_bar, 1))
-        )
+        fields[5] = fields[5] + lacking
+        if part:
+            fields[2] = fields[2] + SUBSTEP * lacking
+    centres[1] = centres[1] + SUBSTEP * centres[4]
+    centres[2] = centres[2] + SUBSTEP * centres[5]
     inner = slice(W, W + ny)
-    return (
-        height[inner, :nx],
-        east_bar[inner, :nx],
-        north_bar[inner, :nx],
-        centres[4][inner],
-        centres[5][inner],
-    )
+    forces = centres[4][inner], centres[5][inner]
+    lines = ny + 2 * W
+    last = WIDTHS[1] - 1
+    given = (lane == last) | (lane == nx - 1 - last)
+    zero = jnp.zeros((8, 2 * nx), jnp.float32)
+    for i in (0, 2):
+        tank[i, :8, :] = zero
+        tank[i, lines + 8 :, :] = zero
+    for half, (height, east_bar, north_bar, water, force_east, force_north) in enumerate((centres, halos)):
+        place = slice(half * nx, (half + 1) * nx)
+        wet = water > 0.0
+        pull = (0.5 * SUBSTEP * GRAVITY / 20.0) * water
+        tank[0, 8 : lines + 8, place] = height
+        tank[1, 8 : lines + 8, place] = jnp.where(wet | given if half else wet, east_bar, 0.0)
+        tank[2, 8 : lines + 8, place] = jnp.where(wet, north_bar, 0.0)
+        tank[3, 8 : lines + 8, place] = pull
+        tank[4, 8 : lines + 8, place] = jnp.where(wet, SUBSTEP * force_east, 0.0)
+        tank[5, 8 : lines + 8, place] = jnp.where(wet, SUBSTEP * force_north, 0.0)
+        tank[6, 8 : lines + 8, place] = jnp.where(wet, 0.5 * SUBSTEP, 0.0)
+        tank[7, 8 : lines + 8, place] = jnp.where(given, 0.0, pull) if half else pull
+
+    def across(x):
+        return roll_lanes(x, 2 * nx - 1) - roll_lanes(x, 1)
+
+    for step in range(NSUB):
+        final = step == NSUB - 1
+        for start in range(8, lines + 8, 8):
+            here, above, below = (pl.ds(start + i, 8) for i in (0, 1, -1))
+            whole = not final or 8 < start < lines
+            if whole:
+                east_bar = tank[1, here] - tank[3 if step else 7, here] * across(tank[0, here])
+                tank[1, here] = east_bar + tank[4, here] if step else east_bar
+            north_bar = tank[2, here] - tank[3, here] * (tank[0, above] - tank[0, below])
+            tank[2, here] = north_bar + tank[5, here] if step else north_bar
+        for start in range(16 if final else 8, lines if final else lines + 8, 8):
+            here, above, below = (pl.ds(start + i, 8) for i in (0, 1, -1))
+            if final:
+                turn = across(tank[1, here])[:, :nx] + (tank[2, above, :nx] - tank[2, below, :nx])
+                tank[0, here, :nx] = tank[0, here, :nx] - tank[6, here, :nx] * turn
+            else:
+                turn = across(tank[1, here]) + (tank[2, above] - tank[2, below])
+                tank[0, here] = tank[0, here] - tank[6, here] * turn
+    mine = pl.ds(8 + W, ny)
+    return tank[0, mine, :nx], tank[1, mine, :nx], tank[2, mine, :nx], *forces
 
 
 def ahead_less_behind(x):
@@ -462,9 +499,8 @@
     shape = (ny, nx)
     lane = lanes_of(shape)
     low = lax.axis_index("ga") == 0
-    tall = ny - FOLD_ROWS
-    from_east = unfold(jnp.where(low, from_first[:tall], from_second[:tall]))
-    from_west = unfold(jnp.where(low, from_second[:tall], from_first[:tall]))
+    from_east = unfold(jnp.where(low, from_first[...], from_second[...]))
+    from_west = unfold(jnp.where(low, from_second[...], from_first[...]))
     spot = rows_of((nx, nx))
     place = lanes_of((nx, nx))
     spread_east = jnp.where((place == 2 * spot) & (spot < FIELD_LANE), 1.0, 0.0)
@@ -532,6 +568,7 @@
     velocity,
     rims,
     shallow,
+    tank,
     sems,
 ):
     depth, ny, nx = mixed.shape
@@ -551,7 +588,7 @@
     base = f_row + pad + 8
     swapped = []
     for block in (from_north, from_south):
-        one, two = block[base : base + 16], block[base + 16 : base + 32]
+        one, two = block[base : base + 8], block[base + 8 : base + 16]
         swapped.append(
             jnp.concatenate([block[:base], jnp.where(low, two, one), jnp.where(low, one, two)], axis=0)
         )
@@ -559,7 +596,7 @@
 
     fields = [surface[...], transport[0], transport[1], levels[...], push_east[...], push_north[...]]
     height, east_bar, north_bar, force_east, force_north = subcycles(
-        fields, packed[...], from_west, from_east, from_south, from_north, own_north, own_south, pad
+        tank, fields, packed[...], from_west, from_east, from_south, from_north, own_north, own_south, pad
     )
     shallow[0] = height
     shallow[1] = east_bar
@@ -661,7 +698,7 @@
     pair = sd((2, depth, ny, nx), f32)
     cells = depth * ny * nx
     plane = sd((ny, nx), f32)
-    edge = sd((ny - FOLD_ROWS + 8, nx), f32)
+    edge = sd((EDGE_ROWS, nx), f32)
     outs = pl.pallas_call(
         functools.partial(edges_kernel, total_rows),
         out_shape=[edge, edge, sd((rows, nx), f32), sd((rows, nx), f32)] + [plane] * 6 + [sd((24, ny, nx), f32)],
@@ -703,11 +740,9 @@
     )(thermal, current, mixing, ground)
     zonal_first, zonal_second, velocity_east = lax.optimization_barrier((zonal_first, zonal_second, velocity_east))
     even = lax.axis_index("gy") % 2 == 0
-    tall = ny - FOLD_ROWS
-    top = [zonal_first[tall - 8 :], zonal_second[tall - 8 :]]
-    bottom = [zonal_first[:8], zonal_first[tall:], zonal_second[:8], zonal_second[tall:]]
-    top = jnp.concatenate(top, axis=0)
-    bottom = jnp.concatenate(bottom, axis=0)
+    end = EDGE_ROWS - 8
+    top = jnp.concatenate([zonal_first[end:], zonal_second[end:]], axis=0)
+    bottom = jnp.concatenate([zonal_first[:8], zonal_second[:8]], axis=0)
     merid_first = partner(jnp.concatenate([to_first, jnp.where(even, top, bottom)], axis=0), False, 0)
     merid_second = partner(jnp.concatenate([to_second, jnp.where(even, bottom, top)], axis=0), False, 1)
     velocity_east, mixed = pl.pallas_call(
@@ -729,6 +764,7 @@
             pltpu.VMEM((2, depth, ny, nx), f32),
             pltpu.VMEM((depth, 16, nx), f32),
             pltpu.VMEM((5, ny, nx), f32),
+            pltpu.VMEM((8, ny + 4 * W, 2 * nx), f32),
             pltpu.SemaphoreType.DMA((5 + GROUPS,)),
         ],
         compiler_params=params,

time: 29.4 us -> 28.3 us (0.963)
  Pallas kernels: 13.1 us -> 12.2 us
    pallas_call x1, Pallas kernels: 3.75 us -> 3.12 us  [per_device(): pl.pallas_call(finish_kernel, out_shape=[cube, pair, sd((ny, nx), f32), s...]
where the time goes in v1:
time: 28.3 us; the launch traced here: 28.2 us
  starting transfers between devices  15 us (53%)
  Pallas kernels  12.2 us (43%)
  between operations  0.74 us (3%)
    ppermute x4, starting transfers between devices, partner(): return lax.ppermute(block, AXES, pairs)  15 us
    pallas_call x1, Pallas kernels, per_device(): pl.pallas_call(functools.partial(columns_kernel, total_rows), out_shape=[...  4.16 us
    pallas_call x1, Pallas kernels, per_device(): pl.pallas_call(functools.partial(edges_kernel, total_rows), out_shape=[ed...  3.44 us
    pallas_call x1, Pallas kernels, per_device(): pl.pallas_call(finish_kernel, out_shape=[cube, pair, sd((ny, nx), f32), s...  3.12 us
    pallas_call x1, Pallas kernels, per_device(): pl.pallas_call(zonal_kernel, out_shape=[cube, cube], in_specs=[here] * 8,...  1.53 us
  transfers between devices with their start and end apart: 4, of which 1 were waited for; matrix products, arithmetic and copies ran while one was open for 0% of the time, Pallas kernels for 20%

profile of v1, /device:TPU:1, one launch (start us, length us, event | category | flops | bytes accessed | tf_op | source)
XLA Modules:
  0.0 28.2 jit_solution(13462712947334329622)
XLA Ops:
  0.6 3.4 %edges.1 = (f32[80,128]{1,0:T(8,128)S(1)}, f32[80,128]{1,0:T(8,128)S(1)}, f32[104,128]{1,0:T(8,128)S(1)}, f32[104,128]{1,0:T(8,128)S(1)}, f32[128,128]{1,0:T(8,1...) custom-call(f32[20,128,128]{2,1,0:T(8,128)} %thermal.3, ...), custom_call_target="tpu_custom_call" | custom-call | flops 9830400 | bytes 3932160 | tf_op jit(solution)/shard_map/edges/pallas_call | solution.py:702
  4.1 7.8 %collective-permute-start = (f32[80,128]{1,0:T(8,128)S(1)}, f32[80,128]{1,0:T(8,128)S(1)}, u32[]{:S(2)}, u32[]{:S(2)}) collective-permute-start(f32[80,128]{1,0:T(8,128)S(1)} %get-tuple-element.34), channel_id=1, source_target_pairs={{0,1},{2,3},{4,5},{6,7},{8,9},{10,11},{12,13},{14,15},{1,0},{3,2},... | collective-permute-start | bytes 122888 | tf_op jit(solution)/shard_map/ppermute | solution.py:680
  11.9 2.3 %collective-permute-start.1 = (f32[80,128]{1,0:T(8,128)S(1)}, f32[80,128]{1,0:T(8,128)S(1)}, u32[]{:S(2)}, u32[]{:S(2)}) collective-permute-start(f32[80,128]{1,0:T(8,128)S(1)} %get-tuple-element.35), channel_id=1, source_target_pairs={{0,241},{2,243},{4,245},{6,247},{8,249},{10,251},{12,253},{14,255}... | collective-permute-start | bytes 122888 | tf_op jit(solution)/shard_map/ppermute | solution.py:680
  14.2 4.2 %columns.1 = (f32[20,128,128]{2,1,0:T(8,128)S(1)}, f32[20,128,128]{2,1,0:T(8,128)S(1)}, f32[20,128,128]{2,1,0:T(8,128)S(1)}, f32[20,128,128]{2,1,0:T(8,128)S(1)}...) custom-call(f32[20,128,128]{2,1,0:T(8,128)} %thermal.3, f32[2,20,128,128]{3,2,1,0:T(8,128)} %current.3, ...), custom_call_target="tpu_custom_call" | custom-call | flops 32768000 | bytes 13107200 | tf_op jit(solution)/shard_map/columns/pallas_call | solution.py:724
  18.3 0.0 collective-permute-done.from_first.zonal_first
  18.4 0.0 collective-permute-done.1.from_second.zonal_second
  18.4 4.8 %collective-permute-start.2 = (f32[120,128]{1,0:T(8,128)S(1)}, f32[120,128]{1,0:T(8,128)S(1)}, u32[]{:S(2)}, u32[]{:S(2)}) collective-permute-start(f32[120,128]{1,0:T(8,128)S(1)} %pad_maximum_fusion), channel_id=1, source_target_pairs={{2,4},{4,2},{6,8},{8,6},{10,12},{12,10},{3,5},{5,3},{7,9},{9,7},{1... | collective-permute-start | bytes 184328 | tf_op jit(solution)/shard_map/ppermute | solution.py:680
  23.2 0.1 collective-permute-start.3
  23.3 0.0 copy-start
  23.3 0.0 copy-start.1
  23.4 1.5 %zonal.1 = (f32[20,128,128]{2,1,0:T(8,128)S(1)}, f32[20,128,128]{2,1,0:T(8,128)S(1)}) custom-call(f32[128,128]{1,0:T(8,128)S(1)} %get-tuple-element.26.levels, f32[80,128]{1,0:T(8,128)S(1)} %collective-permute-done.from_first.zonal_first, f32[80,128]{1,0:T(8,128)S(1)} %collective-permute-done.1.from_second.zonal_second, ...), custom_call_target="tpu_custom_call" | custom-call | flops 6553600 | bytes 6553600 | tf_op jit(solution)/shard_map/zonal/pallas_call | solution.py:748
  24.9 0.2 collective-permute-done.2.merid_second
  25.1 0.0 collective-permute-done.3.merid_first
  25.1 0.0 copy-done
  25.1 0.0 copy-done.1
  25.1 3.1 %finish.1 = (f32[20,128,128]{2,1,0:T(8,128)}, f32[2,20,128,128]{3,2,1,0:T(8,128)}, f32[128,128]{1,0:T(8,128)}, f32[2,128,128]{2,1,0:T(8,128)}) custom-call(f32[128,128]{1,0:T(8,128)S(1)} %get-tuple-element.26.levels, f32[128,128]{1,0:T(8,128)S(1)} %copy-done.1, f32[2,128,128]{2,1,0:T(8,128)S(1)} %copy-done, f32[128,128]{1,0:T(8,128)S(1)} %get-tuple-element.27.sum_east, ...), custom_call_target="tpu_custom_call" | custom-call | tf_op jit(solution)/shard_map/finish/pallas_call | solution.py:758
  (4 shorter events, 0.0 us)
Async XLA Ops:
  4.1 14.3 %collective-permute-start = (f32[80,128]{1,0:T(8,128)S(1)}, f32[80,128]{1,0:T(8,128)S(1)}, u32[]{:S(2)}, u32[]{:S(2)}) collective-permute-start(f32[80,128]{1,0:T(8,128)S(1)} %get-tuple-element.34), channel_id=1, source_target_pairs={{0,1},{2,3},{4,5},{6,7},{8,9},{10,11},{12,13},{14,15},{1,0},{3,2},... | collective-permute-start | bytes 122888 | tf_op jit(solution)/shard_map/ppermute | solution.py:680
  11.9 6.5 %collective-permute-start.1 = (f32[80,128]{1,0:T(8,128)S(1)}, f32[80,128]{1,0:T(8,128)S(1)}, u32[]{:S(2)}, u32[]{:S(2)}) collective-permute-start(f32[80,128]{1,0:T(8,128)S(1)} %get-tuple-element.35), channel_id=1, source_target_pairs={{0,241},{2,243},{4,245},{6,247},{8,249},{10,251},{12,253},{14,255}... | collective-permute-start | bytes 122888 | tf_op jit(solution)/shard_map/ppermute | solution.py:680
  18.4 6.7 %collective-permute-start.2 = (f32[120,128]{1,0:T(8,128)S(1)}, f32[120,128]{1,0:T(8,128)S(1)}, u32[]{:S(2)}, u32[]{:S(2)}) collective-permute-start(f32[120,128]{1,0:T(8,128)S(1)} %pad_maximum_fusion), channel_id=1, source_target_pairs={{2,4},{4,2},{6,8},{8,6},{10,12},{12,10},{3,5},{5,3},{7,9},{9,7},{1... | collective-permute-start | bytes 184328 | tf_op jit(solution)/shard_map/ppermute | solution.py:680
  23.2 1.9 %collective-permute-start.3 = (f32[120,128]{1,0:T(8,128)S(1)}, f32[120,128]{1,0:T(8,128)S(1)}, u32[]{:S(2)}, u32[]{:S(2)}) collective-permute-start(f32[120,128]{1,0:T(8,128)S(1)} %pad_maximum_fusion.1), channel_id=1, source_target_pairs={{0,2},{2,0},{4,6},{6,4},{8,10},{10,8},{12,14},{14,12},{1,3},{3,1},... | collective-permute-start | bytes 184328 | tf_op jit(solution)/shard_map/ppermute | solution.py:680
  23.3 1.8 %copy-start = (f32[2,128,128]{2,1,0:T(8,128)S(1)}, f32[2,128,128]{2,1,0:T(8,128)}, u32[]{:S(2)}) copy-start(f32[2,128,128]{2,1,0:T(8,128)} %transport.3) | copy-start | bytes 393220
  23.3 1.8 %copy-start.1 = (f32[128,128]{1,0:T(8,128)S(1)}, f32[128,128]{1,0:T(8,128)}, u32[]{:S(2)}) copy-start(f32[128,128]{1,0:T(8,128)} %surface.3) | copy-start | bytes 196612

commit v2 on v1

--- a/solution.py
+++ b/solution.py
@@ -584,6 +584,9 @@
 
     from_east, from_west = choose(low, zonal_first, zonal_second)
     from_north, from_south = choose(even, merid_first, merid_second)
+    here = lax.axis_index("gy")
+    from_north = jnp.where(here == lax.axis_size("gy") - 1, 0.0, from_north)
+    from_south = jnp.where(here == 0, 0.0, from_south)
     own_north, own_south = choose(even, own_first.at[pl.ds(p_row, pad)], own_second.at[pl.ds(p_row, pad)])
     base = f_row + pad + 8
     swapped = []
@@ -673,10 +676,9 @@
             if zonal:
                 tx = (x + 1 if x % 2 == parity else x - 1) % count
             else:
-                ty = y + 1 if y % 2 == parity else y - 1
-            if 0 <= ty < sy:
-                source = (x // sa * sy + y) * sa + x % sa
-                pairs.append((source, (tx // sa * sy + ty) * sa + tx % sa))
+                ty = (y + 1 if y % 2 == parity else y - 1) % sy
+            source = (x // sa * sy + y) * sa + x % sa
+            pairs.append((source, (tx // sa * sy + ty) * sa + tx % sa))
     return lax.ppermute(block, AXES, pairs)
 
 

time: 28.3 us -> 26.5 us (0.936)
  starting transfers between devices: 15 us -> 13.1 us
    ppermute x4, starting transfers between devices: 15 us -> 13.1 us  [partner(): return lax.ppermute(block, AXES, pairs)]
  transfers between devices with their start and end apart: 4 -> 4, of which waited for: 1 -> 1; matrix products, arithmetic and copies ran while one was open for 0% -> 0% of each run, Pallas kernels for 20% -> 22%
where the time goes in v2:
time: 26.5 us; the launch traced here: 26.4 us
  starting transfers between devices  13.1 us (49%)
  Pallas kernels  12.3 us (46%)
  between operations  0.72 us (3%)
  waiting for transfers between devices  0.34 us (1%)
    ppermute x4, starting transfers between devices, partner(): return lax.ppermute(block, AXES, pairs)  13.1 us
    pallas_call x1, Pallas kernels, per_device(): pl.pallas_call(functools.partial(columns_kernel, total_rows), out_shape=[...  4.16 us
    pallas_call x1, Pallas kernels, per_device(): pl.pallas_call(functools.partial(edges_kernel, total_rows), out_shape=[ed...  3.44 us
    pallas_call x1, Pallas kernels, per_device(): pl.pallas_call(finish_kernel, out_shape=[cube, pair, sd((ny, nx), f32), s...  3.13 us
    pallas_call x1, Pallas kernels, per_device(): pl.pallas_call(zonal_kernel, out_shape=[cube, cube], in_specs=[here] * 8,...  1.53 us
  transfers between devices with their start and end apart: 4, of which 1 were waited for; matrix products, arithmetic and copies ran while one was open for 0% of the time, Pallas kernels for 22%

profile of v2, /device:TPU:1, one launch (start us, length us, event | category | flops | bytes accessed | tf_op | source)
XLA Modules:
  0.0 26.4 jit_solution(14029083168450563110)
XLA Ops:
  0.6 3.4 %edges.1 = (f32[80,128]{1,0:T(8,128)S(1)}, f32[80,128]{1,0:T(8,128)S(1)}, f32[104,128]{1,0:T(8,128)S(1)}, f32[104,128]{1,0:T(8,128)S(1)}, f32[128,128]{1,0:T(8,1...) custom-call(f32[20,128,128]{2,1,0:T(8,128)} %thermal.3, ...), custom_call_target="tpu_custom_call" | custom-call | flops 9830400 | bytes 3932160 | tf_op jit(solution)/shard_map/edges/pallas_call | solution.py:704
  4.1 7.8 %collective-permute-start = (f32[80,128]{1,0:T(8,128)S(1)}, f32[80,128]{1,0:T(8,128)S(1)}, u32[]{:S(2)}, u32[]{:S(2)}) collective-permute-start(f32[80,128]{1,0:T(8,128)S(1)} %get-tuple-element.34), channel_id=1, source_target_pairs={{0,1},{2,3},{4,5},{6,7},{8,9},{10,11},{12,13},{14,15},{1,0},{3,2},... | collective-permute-start | bytes 122888 | tf_op jit(solution)/shard_map/ppermute | solution.py:682
  11.9 2.3 %collective-permute-start.1 = (f32[80,128]{1,0:T(8,128)S(1)}, f32[80,128]{1,0:T(8,128)S(1)}, u32[]{:S(2)}, u32[]{:S(2)}) collective-permute-start(f32[80,128]{1,0:T(8,128)S(1)} %get-tuple-element.35), channel_id=1, source_target_pairs={{0,241},{2,243},{4,245},{6,247},{8,249},{10,251},{12,253},{14,255}... | collective-permute-start | bytes 122888 | tf_op jit(solution)/shard_map/ppermute | solution.py:682
  14.2 4.2 %columns.1 = (f32[20,128,128]{2,1,0:T(8,128)S(1)}, f32[20,128,128]{2,1,0:T(8,128)S(1)}, f32[20,128,128]{2,1,0:T(8,128)S(1)}, f32[20,128,128]{2,1,0:T(8,128)S(1)}...) custom-call(f32[20,128,128]{2,1,0:T(8,128)} %thermal.3, f32[2,20,128,128]{3,2,1,0:T(8,128)} %current.3, ...), custom_call_target="tpu_custom_call" | custom-call | flops 32768000 | bytes 13107200 | tf_op jit(solution)/shard_map/columns/pallas_call | solution.py:726
  18.3 0.0 collective-permute-done.from_first.zonal_first
  18.4 0.0 collective-permute-done.1.from_second.zonal_second
  18.4 3.0 %collective-permute-start.2 = (f32[120,128]{1,0:T(8,128)S(1)}, f32[120,128]{1,0:T(8,128)S(1)}, u32[]{:S(2)}, u32[]{:S(2)}) collective-permute-start(f32[120,128]{1,0:T(8,128)S(1)} %pad_maximum_fusion), channel_id=1, source_target_pairs={{0,14},{2,4},{4,2},{6,8},{8,6},{10,12},{12,10},{14,0},{1,15},{3,5}... | collective-permute-start | bytes 184328 | tf_op jit(solution)/shard_map/ppermute | solution.py:682
  21.4 0.0 collective-permute-start.3
  21.4 0.0 copy-start
  21.4 0.0 copy-start.1
  21.4 1.5 %zonal.1 = (f32[20,128,128]{2,1,0:T(8,128)S(1)}, f32[20,128,128]{2,1,0:T(8,128)S(1)}) custom-call(f32[128,128]{1,0:T(8,128)S(1)} %get-tuple-element.26.levels, f32[80,128]{1,0:T(8,128)S(1)} %collective-permute-done.from_first.zonal_first, f32[80,128]{1,0:T(8,128)S(1)} %collective-permute-done.1.from_second.zonal_second, ...), custom_call_target="tpu_custom_call" | custom-call | flops 6553600 | bytes 6553600 | tf_op jit(solution)/shard_map/zonal/pallas_call | solution.py:750
  23.0 0.3 %collective-permute-done.2.merid_second = f32[120,128]{1,0:T(8,128)S(1)} collective-permute-done((f32[120,128]{1,0:T(8,128)S(1)}, f32[120,128]{1,0:T(8,128)S(1)}, u32[]{:S(2)}, u32[]{:S(2)}) %collective-permute-start.2) | collective-permute-done | bytes 61472 | tf_op jit(solution)/shard_map/ppermute | solution.py:682
  23.3 0.0 collective-permute-done.3.merid_first
  23.3 0.0 copy-done
  23.3 0.0 copy-done.1
  23.3 3.1 %finish.1 = (f32[20,128,128]{2,1,0:T(8,128)}, f32[2,20,128,128]{3,2,1,0:T(8,128)}, f32[128,128]{1,0:T(8,128)}, f32[2,128,128]{2,1,0:T(8,128)}) custom-call(f32[128,128]{1,0:T(8,128)S(1)} %get-tuple-element.26.levels, f32[128,128]{1,0:T(8,128)S(1)} %copy-done.1, f32[2,128,128]{2,1,0:T(8,128)S(1)} %copy-done, f32[128,128]{1,0:T(8,128)S(1)} %get-tuple-element.27.sum_east, ...), custom_call_target="tpu_custom_call" | custom-call | tf_op jit(solution)/shard_map/finish/pallas_call | solution.py:760
  (4 shorter events, 0.0 us)
Async XLA Ops:
  4.1 14.3 %collective-permute-start = (f32[80,128]{1,0:T(8,128)S(1)}, f32[80,128]{1,0:T(8,128)S(1)}, u32[]{:S(2)}, u32[]{:S(2)}) collective-permute-start(f32[80,128]{1,0:T(8,128)S(1)} %get-tuple-element.34), channel_id=1, source_target_pairs={{0,1},{2,3},{4,5},{6,7},{8,9},{10,11},{12,13},{14,15},{1,0},{3,2},... | collective-permute-start | bytes 122888 | tf_op jit(solution)/shard_map/ppermute | solution.py:682
  11.9 6.5 %collective-permute-start.1 = (f32[80,128]{1,0:T(8,128)S(1)}, f32[80,128]{1,0:T(8,128)S(1)}, u32[]{:S(2)}, u32[]{:S(2)}) collective-permute-start(f32[80,128]{1,0:T(8,128)S(1)} %get-tuple-element.35), channel_id=1, source_target_pairs={{0,241},{2,243},{4,245},{6,247},{8,249},{10,251},{12,253},{14,255}... | collective-permute-start | bytes 122888 | tf_op jit(solution)/shard_map/ppermute | solution.py:682
  18.4 4.9 %collective-permute-start.2 = (f32[120,128]{1,0:T(8,128)S(1)}, f32[120,128]{1,0:T(8,128)S(1)}, u32[]{:S(2)}, u32[]{:S(2)}) collective-permute-start(f32[120,128]{1,0:T(8,128)S(1)} %pad_maximum_fusion), channel_id=1, source_target_pairs={{0,14},{2,4},{4,2},{6,8},{8,6},{10,12},{12,10},{14,0},{1,15},{3,5}... | collective-permute-start | bytes 184328 | tf_op jit(solution)/shard_map/ppermute | solution.py:682
  21.4 1.9 %collective-permute-start.3 = (f32[120,128]{1,0:T(8,128)S(1)}, f32[120,128]{1,0:T(8,128)S(1)}, u32[]{:S(2)}, u32[]{:S(2)}) collective-permute-start(f32[120,128]{1,0:T(8,128)S(1)} %pad_maximum_fusion.1), channel_id=1, source_target_pairs={{0,2},{2,0},{4,6},{6,4},{8,10},{10,8},{12,14},{14,12},{1,3},{3,1},... | collective-permute-start | bytes 184328 | tf_op jit(solution)/shard_map/ppermute | solution.py:682
  21.4 1.9 %copy-start = (f32[2,128,128]{2,1,0:T(8,128)S(1)}, f32[2,128,128]{2,1,0:T(8,128)}, u32[]{:S(2)}) copy-start(f32[2,128,128]{2,1,0:T(8,128)} %transport.3) | copy-start | bytes 393220
  21.4 1.9 %copy-start.1 = (f32[128,128]{1,0:T(8,128)S(1)}, f32[128,128]{1,0:T(8,128)}, u32[]{:S(2)}) copy-start(f32[128,128]{1,0:T(8,128)} %surface.3) | copy-start | bytes 196612
